TPU v7x, 256 devices: a whole 4x4x8 slice. The times are simulated.
256 devices in a mesh: dp: 8 (over z), tensor: 16 (over y, x), segment: 2 (over core).
Axes of the slice: x: 4, y: 4, z: 8, core: 2. Of those that a mesh axis runs over, the one named last changes fastest.
Arguments:
- x_saved: bfloat16 [2, 2, 4096, 2048], P('segment', None, 'dp', 'tensor'), may hold values from -6 to 6
- dy_in: bfloat16 [2, 4096, 2048], P(None, 'dp', 'tensor'), may hold values from -1.5 to 1.5
- w_all: bfloat16 [2, 7168, 3, 2048], P('segment', 'tensor'), may hold values from -0.125 to 0.125
- slot_token: int32 [2, 2, 2048], P('segment', None, 'dp'), may hold values from 0 to 511, as said below
- counts: int32 [2, 2, 8], P('segment', None, 'dp'), may hold values from 129 to 256, as said below
- probs: float32 [2, 2, 2048], P('segment', None, 'dp'), may hold values from 0.1 to 0.6
- adam_m: bfloat16 [2, 44040192], P('segment', ('tensor', 'dp')), may hold values from -24 to 24
- adam_v: bfloat16 [2, 44040192], P('segment', ('tensor', 'dp')), may hold values from 4 to 64
Outputs:
- dx_out: bfloat16 [2, 2, 4096, 2048], P('segment', None, 'dp', 'tensor')
- grad_sum: bfloat16 [2, 44040192], P('segment', ('tensor', 'dp'))
- new_m: bfloat16 [2, 44040192], P('segment', ('tensor', 'dp'))
- new_v: bfloat16 [2, 44040192], P('segment', ('tensor', 'dp'))
- new_w: bfloat16 [2, 44040192], P('segment', ('tensor', 'dp'))
Inputs may be any that keep to these rules, and one draw needn't show every extreme that they name: `slot_token`: within each dp block of a layer and micro-batch the 256 values are distinct and ascending. `counts`: in every layer and micro-batch some dp block has all 256 rows live.
All inputs are finite; a program needn't handle non-finite values.
Results may differ from a plain program's by a relative error of at most 0.019.
Values may be sent and summed in bfloat16 or wider, within the bound.
A program may use at most 128 MiB of HBM per device.

v0:
```python
import jax
import jax.numpy as jnp
from jax import lax
from jax.sharding import PartitionSpec as P

BLOCK = 128


beta_one = 0.9
beta_two = 0.95
learning_rate = 0.01
adam_epsilon = 1e-08
bias_one = 0.9999734386011124
bias_two = 0.994079470779666


def passed_along(value, axis, steps):
    count = lax.axis_size(axis)
    first, last = (max(0, -steps), min(count, count - steps))
    return lax.ppermute(value, axis, [(source, source + steps) for source in range(first, last)])


def from_partner(value, axis, apart):
    return lax.ppermute(value, axis, [(i, i ^ 1 << apart) for i in range(lax.axis_size(axis))])


def contract(left, right, left_dim, right_dim):
    return lax.dot_general(
        left, right, (((left_dim,), (right_dim,)), ((), ())), preferred_element_type=jnp.float32
    )


def pick_rows(table, positions):
    return jnp.take(table, positions, axis=0)


def local(x_saved, dy_in, w_all, slot_token, counts, probs, adam_m, adam_v):
    segment_count = lax.axis_size("segment")
    segment_pos = lax.axis_index("segment")
    dp_count = lax.axis_size("dp")
    dp_pos = lax.axis_index("dp")
    weights = w_all[0]
    gate_w = weights[:, 0, :]
    up_w = weights[:, 1, :]
    down_w = weights[:, 2, :]
    micro_count, tok_count, narrow = dy_in.shape
    slot_count = slot_token.shape[2]
    hidden_dev = weights.shape[0]
    model_width = weights.shape[2]
    token_rows = slot_token[0]
    live_counts = counts[0, :, 0]
    positions = jnp.arange(slot_count, dtype=jnp.int32)
    gating = jnp.where(positions[None, :] < live_counts[:, None], probs[0], 0.0)
    saved = x_saved[0]
    full_inputs = lax.all_gather(saved, "tensor", axis=2, tiled=True)
    input_rows = jax.vmap(pick_rows)(full_inputs, token_rows)
    accum = jnp.zeros((hidden_dev, 3, model_width), jnp.float32)
    received = jnp.zeros((tok_count, narrow), jnp.bfloat16)
    results = jnp.zeros((micro_count, tok_count, narrow), jnp.bfloat16)
    tick_count = micro_count + segment_count - 1
    batch_ids = jnp.arange(micro_count, dtype=jnp.int32)
    for moment in range(tick_count):
        batch_index = moment - (segment_count - 1) + segment_pos
        is_active = (batch_index >= 0) & (batch_index < micro_count)
        clipped = jnp.clip(batch_index, 0, micro_count - 1)
        upstream = jnp.where(
            segment_pos == segment_count - 1, dy_in[min(moment, micro_count - 1)], received
        )
        row_tokens = lax.dynamic_index_in_dim(token_rows, clipped, 0, False)
        row_gates = lax.dynamic_index_in_dim(gating, clipped, 0, False)
        inputs = lax.dynamic_index_in_dim(input_rows, clipped, 0, False)
        upstream_full = lax.all_gather(upstream, "tensor", axis=1, tiled=True)
        picked_grad = pick_rows(upstream_full, row_tokens)
        scaled = (row_gates[:, None] * picked_grad.astype(jnp.float32)).astype(jnp.bfloat16)
        live_now = lax.dynamic_index_in_dim(live_counts, clipped, 0, False)
        live_blocks = jnp.where(is_active, (live_now + BLOCK - 1) // BLOCK, 0)

        def block_step(block_no, state_pair):
            grads_acc, partial_value = state_pair
            row_start = block_no * BLOCK
            input_block = lax.dynamic_slice_in_dim(inputs, row_start, BLOCK, 0)
            grad_block = lax.dynamic_slice_in_dim(scaled, row_start, BLOCK, 0)
            gate_pre = contract(input_block, gate_w, 1, 1)
            up_pre = contract(input_block, up_w, 1, 1)
            sigmoid_g = jax.nn.sigmoid(gate_pre)
            active = gate_pre * sigmoid_g
            hidden = (active * up_pre).astype(jnp.bfloat16)
            hidden_grad = contract(grad_block, down_w, 1, 1)
            d_gate = (
                hidden_grad * up_pre * sigmoid_g * (1.0 + gate_pre * (1.0 - sigmoid_g))
            ).astype(jnp.bfloat16)
            d_up = (hidden_grad * active).astype(jnp.bfloat16)
            back = jnp.dot(d_gate, gate_w, preferred_element_type=jnp.float32)
            back = back + jnp.dot(d_up, up_w, preferred_element_type=jnp.float32)
            gate_grad = contract(d_gate, input_block, 0, 0)
            up_grad = contract(d_up, input_block, 0, 0)
            down_grad = contract(hidden, grad_block, 0, 0)
            grads_acc = grads_acc + jnp.stack([gate_grad, up_grad, down_grad], axis=1)
            partial_value = lax.dynamic_update_slice_in_dim(partial_value, back, row_start, 0)
            return (grads_acc, partial_value)

        start_partial = jnp.zeros((slot_count, model_width), jnp.float32)
        accum, partial_value = lax.fori_loop(0, live_blocks, block_step, (accum, start_partial))
        spread = jnp.zeros((tok_count, model_width), jnp.float32).at[row_tokens].add(partial_value)
        summed = lax.psum_scatter(
            spread.astype(jnp.bfloat16), "tensor", scatter_dimension=1, tiled=True
        ).astype(jnp.float32)
        gradient = (upstream.astype(jnp.float32) + summed).astype(jnp.bfloat16)
        chosen = is_active & (batch_ids == clipped)
        results = jnp.where(chosen[:, None, None], gradient[None], results)
        if moment < tick_count - 1:
            received = passed_along(gradient, "segment", -1)
    pieces = accum.astype(jnp.bfloat16).reshape(dp_count, -1)
    piece_len = pieces.shape[1]
    level_count = dp_count.bit_length() - 1
    low_bit = dp_pos % 2
    paired = pieces.reshape(dp_count // 2, 2, piece_len)
    kept_half = lax.dynamic_index_in_dim(paired, low_bit, 1, False)
    sent_half = lax.dynamic_index_in_dim(paired, 1 - low_bit, 1, False)
    partner_half = from_partner(sent_half, "dp", 0)
    running = kept_half.astype(jnp.float32) + partner_half.astype(jnp.float32)
    for level_bit in range(1, level_count):
        own_bit = dp_pos // 2**level_bit % 2
        halves = running.reshape(running.shape[0] // 2, 2, piece_len)
        own_half = lax.dynamic_index_in_dim(halves, own_bit, 1, False)
        other_half = lax.dynamic_index_in_dim(halves, 1 - own_bit, 1, False)
        running = own_half + from_partner(other_half.astype(jnp.bfloat16), "dp", level_bit).astype(
            other_half.dtype
        )
    reduced = running[0]
    grad_piece = reduced.astype(jnp.bfloat16)
    grad_value = grad_piece.astype(jnp.float32)
    moment_one = beta_one * adam_m[0].astype(jnp.float32) + (1.0 - beta_one) * grad_value
    moment_two = (
        beta_two * adam_v[0].astype(jnp.float32) + (1.0 - beta_two) * grad_value * grad_value
    )
    own_weights = lax.dynamic_index_in_dim(weights.reshape(dp_count, -1), dp_pos, 0, False).astype(
        jnp.float32
    )
    update = moment_one / bias_one / (jnp.sqrt(moment_two / bias_two) + adam_epsilon)
    new_weight = own_weights - learning_rate * update
    return (
        results[None],
        grad_piece[None],
        moment_one.astype(jnp.bfloat16)[None],
        moment_two.astype(jnp.bfloat16)[None],
        new_weight.astype(jnp.bfloat16)[None],
    )


def solution(mesh):
    return jax.shard_map(
        local,
        mesh=mesh,
        in_specs=(
            P("segment", None, "dp", "tensor"),
            P(None, "dp", "tensor"),
            P("segment", "tensor", None, None),
            P("segment", None, "dp"),
            P("segment", None, "dp"),
            P("segment", None, "dp"),
            P("segment", ("tensor", "dp")),
            P("segment", ("tensor", "dp")),
        ),
        out_specs=(
            P("segment", None, "dp", "tensor"),
            P("segment", ("tensor", "dp")),
            P("segment", ("tensor", "dp")),
            P("segment", ("tensor", "dp")),
            P("segment", ("tensor", "dp")),
        ),
        check_vma=False,
    )
```

profile of v0, /device:TPU:2, one launch (start us, length us, event | category | flops | bytes accessed | tf_op | source)
XLA Modules:
  0.0 825.4 jit_solution(3805622791041290404)
XLA Ops:
  21.2 45.1 %all-gather.11.cloned.1.call-done = bf16[1,512,2048]{2,1,0:T(8,128)(2,1)} async-done(((bf16[1,512,128]{2,1,0:T(8,128)(2,1)}), bf16[1,512,2048]{2,1,0:T(8,128)(2,1)}) %all-gather.11.cloned.1.call-update) | async-done | bytes 2097168 | tf_op jit(solution)/shard_map/all_gather | solution.py:72
  71.8 58.9 %all-gather.13.cloned.1.call-done = bf16[1,2,512,2048]{3,2,1,0:T(8,128)(2,1)} async-done(((bf16[1,2,512,128]{3,2,1,0:T(8,128)(2,1)}), bf16[1,2,512,2048]{3,2,1,0:T(8,128)(2,1)}) %all-gather.13.cloned.1.call-update) | async-done | bytes 4194320 | tf_op jit(solution)/shard_map/all_gather | solution.py:55
  130.8 13.0 %gather_fusion = bf16[512,2048]{1,0:T(8,128)(2,1)} fusion(bf16[2,512,2048]{2,1,0:T(8,128)(2,1)} %bitcast.192, s32[512]{0:T(512)S(1)} %bitcast.193), kind=kCustom, calls=%fused_computation.3 | custom fusion | bytes 4198400 | tf_op jit(solution)/shard_map/vmap(jit(_take))/gather | solution.py:34
  154.6 6.9 scatter_custom_fusion
  169.3 110.9 %reduce-scatter.10.cloned.1.call-done = bf16[128,512]{1,0:T(8,128)(2,1)} async-done(((bf16[2048,512]{1,0:T(8,128)(2,1)}), bf16[128,512]{1,0:T(8,128)(2,1)}) %reduce-scatter.10.cloned.1.call-update) | async-done | bytes 131088
  286.5 51.5 %all-gather.7.cloned.1.call-done = bf16[512,2048]{1,0:T(8,128)(2,1)} async-done(((bf16[512,128]{1,0:T(8,128)(2,1)}), bf16[512,2048]{1,0:T(8,128)(2,1)}) %all-gather.7.cloned.1.call-update) | async-done | bytes 2097168 | tf_op jit(solution)/shard_map/all_gather | solution.py:72
  347.3 32.8 %while.37 = (s32[]{:T(128)}, f32[448,3,2048]{2,0,1:T(8,128)}, f32[256,2048]{1,0:T(8,128)}, s32[]{:T(128)}, bf16[256,2048]{1,0:T(8,128)(2,1)}, /*index=5*/bf16[44...) while((s32[]{:T(128)}, f32[448,3,2048]{2,0,1:T(8,128)}, ...), condition=%wide.region_5.7_spmd, body=%wide.region_4.6_spmd.sunk | while | flops 1888657408 | bytes 170328496 | solution.py:103
  380.1 6.9 scatter_custom_fusion.1
  394.8 78.9 %reduce-scatter.12.cloned.1.call-done = bf16[128,512]{1,0:T(8,128)(2,1)} async-done(((bf16[2048,512]{1,0:T(8,128)(2,1)}), bf16[128,512]{1,0:T(8,128)(2,1)}) %reduce-scatter.12.cloned.1.call-update) | async-done | bytes 131088
  479.8 51.2 %all-gather.9.cloned.1.call-done = bf16[512,2048]{1,0:T(8,128)(2,1)} async-done(((bf16[512,128]{1,0:T(8,128)(2,1)}), bf16[512,2048]{1,0:T(8,128)(2,1)}) %all-gather.9.cloned.1.call-update) | async-done | bytes 2097168 | tf_op jit(solution)/shard_map/all_gather | solution.py:72
  540.4 32.6 %while.38 = (s32[]{:T(128)}, f32[448,3,2048]{2,0,1:T(8,128)}, f32[256,2048]{1,0:T(8,128)}, s32[]{:T(128)}, bf16[256,2048]{1,0:T(8,128)(2,1)}, /*index=5*/bf16[44...) while((s32[]{:T(128)}, f32[448,3,2048]{2,0,1:T(8,128)}, ...), condition=%wide.region_9.11_spmd, body=%wide.region_8.10_spmd.sunk | while | flops 1888657408 | bytes 170328496 | solution.py:103
  573.1 7.4 convert_element_type.167
  580.5 10.2 %copy.18 = bf16[448,3,2048]{2,1,0:T(4,128)(2,1)} copy(bf16[448,3,2048]{2,0,1:T(8,128)(2,1)} %convert_element_type.167) | data formatting | bytes 11010048 | tf_op jit(solution)/shard_map/convert_element_type | solution.py:113
  590.7 10.2 %reshape_reshape.3 = bf16[4,2,344064]{2,1,0:T(2,128)(2,1)} reshape(bf16[448,3,2048]{2,1,0:T(4,128)(2,1)} %copy.18) | data formatting | bytes 11010048 | tf_op jit(solution)/shard_map/reshape;reshape | solution.py:117
  600.8 12.5 %constant_dynamic-slice_fusion.1 = (bf16[4,1,344064]{2,1,0:T(2,128)(2,1)S(1)}, f32[4,1,344064]{2,1,0:T(1,128)}) fusion(bf16[4,2,344064]{2,1,0:T(2,128)(2,1)} %reshape_reshape.3, s32[]{:T(128)S(6)} %select_n.234, s32[]{:T(128)S(6)} %select_n.233), kind=kLoop, calls=%fused_computation.131 | loop fusion | flops 1376256 | bytes 13762568 | tf_op jit(solution)/shard_map/jit(dynamic_index_in_dim)/dynamic_slice | solution.py:119
  613.3 6.6 copy.35
  621.9 10.2 %copy.19 = bf16[1,448,3,2048]{3,2,1,0:T(4,128)(2,1)} copy(bf16[1,448,3,2048]{3,1,2,0:T(8,128)(2,1)} %param.18) | data formatting | bytes 11010048 | tf_op args[2]
  632.1 12.9 %reshape_squeeze.3 = bf16[8,344064]{1,0:T(8,128)(2,1)} reshape(bf16[1,448,3,2048]{3,2,1,0:T(4,128)(2,1)} %copy.19) | data formatting | bytes 11010048 | tf_op jit(solution)/shard_map/reshape;squeeze | solution.py:137
  645.0 7.0 scatter_custom_fusion.2
  659.8 9.2 %bitcast_add_fusion = f32[4,344064]{1,0:T(4,128)} fusion(f32[4,1,344064]{2,1,0:T(1,128)} %get-tuple-element.231, bf16[4,344064]{1,0:T(4,128)(2,1)} %collective-permute-done.2), kind=kLoop, calls=%fused_computation.88 | loop fusion | flops 2752512 | bytes 13762560 | tf_op jit(solution)/shard_map/add | solution.py:121
  669.0 9.3 %reshape.201 = f32[2,2,344064]{2,1,0:T(2,128)} reshape(f32[4,344064]{1,0:T(4,128)} %bitcast_add_fusion) | data formatting | bytes 11010048 | tf_op jit(solution)/shard_map/reshape | solution.py:124
  694.3 57.8 %collective-permute-done.3 = bf16[2,344064]{1,0:T(2,128)(2,1)S(1)} collective-permute-done((bf16[2,344064]{1,0:T(2,128)(2,1)S(1)}, bf16[2,344064]{1,0:T(2,128)(2,1)S(1)}, u32[]{:S(2)}, u32[]{:S(2)}) %collective-permute-start.3) | collective-permute-done | bytes 1376288 | tf_op jit(solution)/shard_map/ppermute | solution.py:24
  767.4 30.6 %collective-permute-done.4 = bf16[1,344064]{1,0:T(2,128)(2,1)} collective-permute-done((bf16[1,344064]{1,0:T(2,128)(2,1)}, bf16[1,344064]{1,0:T(2,128)(2,1)}, u32[]{:S(2)}, u32[]{:S(2)}) %collective-permute-start.4) | collective-permute-done | bytes 688160 | tf_op jit(solution)/shard_map/ppermute | solution.py:24
  798.0 13.7 %subtract_convert_fusion = (bf16[1,344064]{1,0:T(2,128)(2,1)}, bf16[1,344064]{1,0:T(2,128)(2,1)S(1)}) fusion(bf16[8,344064]{1,0:T(8,128)(2,1)} %reshape_squeeze.3, s32[]{:T(128)S(6)} %select_n.243, bf16[1,344064]{1,0:T(2,128)(2,1)S(1)} %copy-done.13, bf16[1,344064]{1,0:T(2,128)(2,1)S(1)} %copy-done.14, bf16[1,344064]{1,0:T(2,128)(2,1)} %collective-permute-done.4, ...), kind=kLoop, calls=%fused_computation.109 | loop fusion | flops 7225344 | bytes 5505032 | tf_op jit(solution)/shard_map/convert_element_type | solution.py:147
  (207 shorter events, 186.9 us)
Async XLA Ops:
  7.2 59.2 %all-gather.11.cloned.1.call-start = ((), (), s32[]{:S(2)}) async-start(), calls=%async_computation.5 | async-start | bytes 2228224 | tf_op jit(solution)/shard_map/all_gather | solution.py:72
  8.8 122.0 %all-gather.13.cloned.1.call-start = ((), (), s32[]{:S(2)}) async-start(), calls=%async_computation.6 | async-start | bytes 4456448 | tf_op jit(solution)/shard_map/all_gather | solution.py:55
  9.6 270.6 %reduce-scatter.10.cloned.1.call-start = ((), (), s32[]{:S(2)}) async-start(), calls=%async_computation.7 | async-start | bytes 2228224
  169.2 112.0 %copy-start.24 = (bf16[2,512,128]{2,1,0:T(8,128)(2,1)S(1)}, bf16[2,512,128]{2,1,0:T(8,128)(2,1)}, u32[]{:S(2)}) copy-start(bf16[2,512,128]{2,1,0:T(8,128)(2,1)} %param.17) | copy-start | bytes 786436
  169.2 168.8 %all-gather.7.cloned.1.call-start = ((), (), s32[]{:S(2)}) async-start(), calls=%async_computation.3 | async-start | bytes 2228224 | tf_op jit(solution)/shard_map/all_gather | solution.py:72
  281.9 3.2 collective-permute-start
  285.8 187.9 %reduce-scatter.12.cloned.1.call-start = ((), (), s32[]{:S(2)}) async-start(), calls=%async_computation.8 | async-start | bytes 2228224
  363.9 7.9 slice-start.3
  394.8 80.0 %copy-start.23 = (bf16[512,128]{1,0:T(8,128)(2,1)S(1)}, bf16[512,128]{1,0:T(8,128)(2,1)}, u32[]{:S(2)}) copy-start(bf16[512,128]{1,0:T(8,128)(2,1)} %bitcast_select_fusion.1) | copy-start | bytes 393220
  394.8 85.0 %copy-start.28 = (s32[1,1,256]{2,1,0:T(1,128)S(1)}, s32[1,1,256]{2,1,0:T(1,128)}, u32[]{:S(2)}) copy-start(s32[1,1,256]{2,1,0:T(1,128)} %get-tuple-element.216) | copy-start | bytes 3076
  394.8 136.2 %all-gather.9.cloned.1.call-start = ((), (), s32[]{:S(2)}) async-start(), calls=%async_computation.4 | async-start | bytes 2228224 | tf_op jit(solution)/shard_map/all_gather | solution.py:72
  474.8 3.2 collective-permute-start.1
  478.8 286.7 %reduce-scatter.14.cloned.1.call-start = ((), (), s32[]{:S(2)}) async-start(), calls=%async_computation.9 | async-start | bytes 2228224
  479.8 56.4 %copy-start.27 = (f32[1,256]{1,0:T(1,128)S(1)}, f32[1,256]{1,0:T(1,128)}, u32[]{:S(2)}) copy-start(f32[1,256]{1,0:T(1,128)} %get-tuple-element.240) | copy-start | bytes 3076
  540.4 7.9 slice-start.6
  556.7 7.9 slice-start.6
  619.9 39.9 %collective-permute-start.2 = (bf16[4,344064]{1,0:T(4,128)(2,1)}, bf16[4,344064]{1,0:T(4,128)(2,1)}, u32[]{:S(2)}, u32[]{:S(2)}) collective-permute-start(bf16[4,344064]{1,0:T(4,128)(2,1)} %bitcast.112), channel_id=1, source_target_pairs={{0,32},{32,0},{64,96},{96,64},{128,160},{160,128},{192,224},{224,1... | collective-permute-start | bytes 8257544 | tf_op jit(solution)/shard_map/ppermute | solution.py:24
  678.3 13.1 %copy-start.11 = (f32[2,2,344064]{2,1,0:T(2,128)S(1)}, f32[2,2,344064]{2,1,0:T(2,128)}, u32[]{:S(2)}) copy-start(f32[2,2,344064]{2,1,0:T(2,128)} %reshape.201) | copy-start | bytes 16515076
  688.8 63.3 %collective-permute-start.3 = (bf16[2,344064]{1,0:T(2,128)(2,1)S(1)}, bf16[2,344064]{1,0:T(2,128)(2,1)S(1)}, u32[]{:S(2)}, u32[]{:S(2)}) collective-permute-start(bf16[2,344064]{1,0:T(2,128)(2,1)S(1)} %bitcast.200), channel_id=1, source_target_pairs={{0,64},{32,96},{64,0},{96,32},{128,192},{160,224},{192,128},{224,1... | collective-permute-start | bytes 4128776 | tf_op jit(solution)/shard_map/ppermute | solution.py:24
  757.9 8.6 %copy-start.22 = (bf16[512,128]{1,0:T(8,128)(2,1)S(1)}, bf16[512,128]{1,0:T(8,128)(2,1)}, u32[]{:S(2)}) copy-start(bf16[512,128]{1,0:T(8,128)(2,1)} %bitcast_select_fusion) | copy-start | bytes 393220
  757.9 8.7 %copy-start.26 = (bf16[512,128]{1,0:T(8,128)(2,1)S(1)}, bf16[512,128]{1,0:T(8,128)(2,1)}, u32[]{:S(2)}) copy-start(bf16[512,128]{1,0:T(8,128)(2,1)} %copy-done.25) | copy-start | bytes 393220
  757.9 40.1 %copy-start.13 = (bf16[1,344064]{1,0:T(2,128)(2,1)S(1)}, bf16[1,344064]{1,0:T(2,128)(2,1)}, u32[]{:S(2)}) copy-start(bf16[1,344064]{1,0:T(2,128)(2,1)} %param.22) | copy-start | bytes 2064388
  757.9 40.1 %copy-start.14 = (bf16[1,344064]{1,0:T(2,128)(2,1)S(1)}, bf16[1,344064]{1,0:T(2,128)(2,1)}, u32[]{:S(2)}) copy-start(bf16[1,344064]{1,0:T(2,128)(2,1)} %param.23) | copy-start | bytes 2064388
  760.3 37.7 %collective-permute-start.4 = (bf16[1,344064]{1,0:T(2,128)(2,1)}, bf16[1,344064]{1,0:T(2,128)(2,1)}, u32[]{:S(2)}, u32[]{:S(2)}) collective-permute-start(bf16[1,344064]{1,0:T(2,128)(2,1)} %dynamic-slice_convert_fusion.2), channel_id=1, source_target_pairs={{0,128},{32,160},{64,192},{96,224},{128,0},{160,32},{192,64},{224,... | collective-permute-start | bytes 2064392 | tf_op jit(solution)/shard_map/ppermute | solution.py:24
  (33 other events, 101.2 us)
Sparse Core Ops, SparseCore 0:
  11.0 55.3 all-gather.10
  68.7 62.0 all-gather.12
  169.4 110.7 reduce-scatter.9
  285.9 52.0 all-gather.6
  394.9 78.8 reduce-scatter.11
  478.9 52.0 all-gather.8
  659.9 77.8 reduce-scatter.13
where the time goes:
time: 835 us; the launch traced here: 825 us
  waiting for transfers between devices  490 us (59%)
  local copies, waits for them, and re-layouts  160 us (19%)
  other arithmetic  113 us (14%)
  matrix products  31.7 us (4%)
  between operations  16.6 us (2%)
  starting transfers between devices  12.8 us (2%)
    unnamed x10, waiting for transfers between devices  191 us
    all_gather x3, waiting for transfers between devices, local(): upstream_full = lax.all_gather(upstream, 'tensor', axis=1, tiled=True)  148 us
    ppermute x3, waiting for transfers between devices, from_partner(): lax.ppermute(value, axis, [(i, i ^ 1 << apart) for i in range(lax.axis_si...  88.4 us
    all_gather x1, waiting for transfers between devices, local(): full_inputs = lax.all_gather(saved, 'tensor', axis=2, tiled=True)  58.9 us
    unnamed x36, local copies, waits for them, and re-layouts  38.5 us
    dot_general x24, matrix products, contract(): lax.dot_general(left, right, (((left_dim,), (right_dim,)), ((), ())), pre...  27.9 us
    gather x4, local copies, waits for them, and re-layouts, pick_rows(): return jnp.take(table, positions, axis=0)  27.6 us
    while x64, local copies, waits for them, and re-layouts  21.3 us
  transfers between devices with their start and end apart: 12, of which 10 were waited for; matrix products, arithmetic and copies ran while one was open for 11% of the time, Pallas kernels for 0%

commit v1 on v0

v1 whole, which is shorter than its diff:
```python
import functools

import jax
import jax.numpy as jnp
from jax import lax
from jax.experimental import pallas as pl
from jax.experimental.pallas import tpu as pltpu
from jax.sharding import PartitionSpec as P

beta_one = 0.9
beta_two = 0.95
learning_rate = 0.01
adam_epsilon = 1e-08
bias_one = 0.9999734386011124
bias_two = 0.994079470779666

MESH = pl.DeviceIdType.MESH
BF = jnp.bfloat16
F32 = jnp.float32
N_DP = 8
N_TENSOR = 16
WIDE = 128
D = N_TENSOR * WIDE
ROWS = 256
TOK = 512
HID = 448
PAD = 512
PIECE = HID // N_DP
HALF = D // 2
QUAR = D // 4
STACK = 2 * PIECE


def dot(left, right, left_dim, right_dim):
    return lax.dot_general(
        left, right, (((left_dim,), (right_dim,)), ((), ())), preferred_element_type=F32
    )


def kernel(x_ref, dy_ref, pick_ref, gate_ref, w_ref, dx_ref, g_ref,
           w, picks, gates, xr, xd, act, coef, hid, dg, du, trans, back, rs,
           gsend, gown, grecv, first, ring, gsum, goth, dxs, dxoth, upd,
           own_sem, w_sem, pg_sem, xr_sem, ag_send, ag_recv, rs_send, rs_recv,
           gx_sem, first_sem, ring_send, ring_recv, gs_sem, dx_sem):
    me_d, me_t, me_c = lax.axis_index("dp"), lax.axis_index("tensor"), lax.axis_index("segment")
    other = 1 - me_c
    my_cols = pl.ds(pl.multiple_of(me_t * WIDE, WIDE), WIDE)

    def at_tensor(n):
        return (me_d, n, me_c)

    def at_dp(n):
        return (n, me_t, me_c)

    partner = (me_d, me_t, other)
    up_d, down_d = lax.rem(me_d + 1, N_DP), lax.rem(me_d + N_DP - 1, N_DP)

    def peer(k):
        return ((me_t // 4 + k // 4) % 4) * 4 + (me_t % 4 + k % 4) % 4

    barrier = pltpu.get_barrier_semaphore()

    def greet(k, carry):
        pl.semaphore_signal(barrier, inc=1, device_id=at_tensor(peer(k)), device_id_type=MESH)
        return carry
    lax.fori_loop(1, N_TENSOR, greet, 0)
    pl.semaphore_signal(barrier, inc=1, device_id=partner, device_id_type=MESH)
    pl.semaphore_signal(barrier, inc=1, device_id=at_dp(up_d), device_id_type=MESH)
    pl.semaphore_signal(barrier, inc=1, device_id=at_dp(down_d), device_id_type=MESH)

    own_w = pltpu.make_async_copy(w_ref, w.at[me_c, :, pl.ds(0, HID)], own_sem.at[0])
    own_w.start()
    for layer in range(2):
        for kind in range(3):
            w[layer, kind, HID:PAD, :] = jnp.zeros((PAD - HID, D), BF)
    picks[me_c] = pick_ref[me_c]
    gates[me_c] = gate_ref[me_c]

    def rows_of(micro):
        choice = pick_ref[micro]
        picked = dot(choice, x_ref[micro], 1, 0)
        grads = gate_ref[micro] * dot(choice, dy_ref[micro], 1, 0)
        return picked.astype(BF), grads.astype(BF)

    there = rows_of(other)
    xr[2, 0] = there[0]
    xr[2, 1] = there[1]
    here = rows_of(me_c)
    xr[me_c, 0] = here[0]
    xr[me_c, 1] = here[1]

    pl.semaphore_wait(barrier, N_TENSOR + 2)

    def to_partner(src, dst, sems, index=None):
        send = sems.at[0] if index is None else sems.at[0, index]
        recv = sems.at[1] if index is None else sems.at[1, index]
        return pltpu.make_async_remote_copy(
            src_ref=src, dst_ref=dst, send_sem=send, recv_sem=recv,
            device_id=partner, device_id_type=MESH)

    xr_copy = to_partner(xr.at[2], xr.at[me_c], xr_sem)
    xr_copy.start()
    w_copy = to_partner(w_ref, w.at[me_c, :, pl.ds(0, HID)], w_sem)
    w_copy.start()
    pick_copy = to_partner(pick_ref.at[other], picks.at[me_c], pg_sem, 0)
    pick_copy.start()
    gate_copy = to_partner(gate_ref.at[other], gates.at[me_c], pg_sem, 1)
    gate_copy.start()

    def gather_copy(src, dst, use, n, owner):
        columns = pl.ds(pl.multiple_of(owner * WIDE, WIDE), WIDE)
        return pltpu.make_async_remote_copy(
            src_ref=src, dst_ref=dst(columns), send_sem=ag_send.at[use, n],
            recv_sem=ag_recv.at[use, owner], device_id=at_tensor(n), device_id_type=MESH)

    def gather_start(src, dst, use):
        def step(k, carry):
            gather_copy(src, dst, use, peer(k), me_t).start()
            return carry
        lax.fori_loop(1, N_TENSOR, step, 0)

    def gather_wait(src, dst, use):
        def step(k, carry):
            n = peer(k)
            gather_copy(src, dst, use, n, n).wait_recv()
            gather_copy(src, dst, use, n, me_t).wait_send()
            return carry
        lax.fori_loop(1, N_TENSOR, step, 0)

    def both_of_one(columns):
        return xd.at[1, :, :, columns]

    def inputs_of_zero(columns):
        return xd.at[0, 0, :, columns]

    def grads_of_zero(columns):
        return xd.at[0, 1, :, columns]

    xr_copy.wait()
    gather_start(xr.at[1], both_of_one, 0)
    gather_start(xr.at[0, 0], inputs_of_zero, 1)
    for kind in range(2):
        xd[1, kind, :, my_cols] = xr[1, kind]
    xd[0, 0, :, my_cols] = xr[0, 0]
    own_w.wait()
    w_copy.wait()
    pick_copy.wait()
    gate_copy.wait()

    def forward(layer):
        def step(block, carry):
            span = pl.ds(pl.multiple_of(block * 256, 256), 256)
            inputs = xd[layer, 0]
            gate_pre = dot(inputs, w[layer, 0, span, :], 1, 1)
            up_pre = dot(inputs, w[layer, 1, span, :], 1, 1)
            sig = 1.0 / (1.0 + jnp.exp(-gate_pre))
            active = gate_pre * sig
            act[:, span] = active
            coef[:, span] = up_pre * sig * (1.0 + gate_pre * (1.0 - sig))
            hid[:, span] = (active * up_pre).astype(BF)
            return carry
        lax.fori_loop(0, PAD // 256, step, 0)

    def hidden_grads(layer):
        def step(block, carry):
            span = pl.ds(pl.multiple_of(block * 256, 256), 256)
            grad = dot(xd[layer, 1], w[layer, 2, span, :], 1, 1)
            dg[:, span] = (grad * coef[:, span]).astype(BF)
            du[:, span] = (grad * act[:, span]).astype(BF)
            return carry
        lax.fori_loop(0, PAD // 256, step, 0)

    def scatter_copy(layer, n, owner):
        return pltpu.make_async_remote_copy(
            src_ref=back.at[layer, n], dst_ref=rs.at[layer, owner],
            send_sem=rs_send.at[layer, n], recv_sem=rs_recv.at[layer, owner],
            device_id=at_tensor(n), device_id_type=MESH)

    def row_grads(layer):
        def step(index, carry):
            pair = lax.rem(me_t // 2 + 1 + index, N_TENSOR // 2)
            span = pl.ds(pl.multiple_of(pair * 256, 256), 256)
            term = dot(dg[...], w[layer, 0, :, span], 1, 0)
            term = (term + dot(du[...], w[layer, 1, :, span], 1, 0)).astype(BF)
            for side in range(2):
                n = pair * 2 + side
                back[layer, n] = term[:, side * WIDE:(side + 1) * WIDE]

                @pl.when(n != me_t)
                def _():
                    scatter_copy(layer, n, me_t).start()
            return carry
        lax.fori_loop(0, N_TENSOR // 2, step, 0)

    def summed_rows(layer):
        def step(k, total):
            n = peer(k)
            scatter_copy(layer, n, n).wait_recv()
            scatter_copy(layer, n, me_t).wait_send()
            return total + rs[layer, n].astype(F32)
        return lax.fori_loop(1, N_TENSOR, step, back[layer, me_t].astype(F32))

    def to_tokens(layer, upstream):
        total = summed_rows(layer)
        high = total.astype(BF)
        low = (total - high.astype(F32)).astype(BF)
        spread = dot(picks[layer], high, 0, 0) + dot(picks[layer], low, 0, 0)
        dxs[layer] = (upstream.astype(F32) + spread).astype(BF)

    def weight_half(layer, half, dst, send):
        def step(kind, carry):
            parts = []
            for quarter in range(2):
                span = pl.ds(pl.multiple_of(half * HALF + quarter * QUAR, QUAR), QUAR)
                parts.append(dot(trans[kind], xd[layer, kind // 2, :, span], 1, 0))
            for d in range(N_DP):
                rows = slice(d * PIECE, (d + 1) * PIECE)
                both = jnp.concatenate([parts[0][rows], parts[1][rows]], axis=0)
                dst[layer, kind, d] = both.astype(BF)
            if send:
                pair_copy(layer, kind).start()
            return carry
        lax.fori_loop(0, 3, step, 0)

    def pair_copy(layer, kind):
        return pltpu.make_async_remote_copy(
            src_ref=gsend.at[layer, kind], dst_ref=grecv.at[layer, kind],
            send_sem=gx_sem.at[0, layer, kind], recv_sem=gx_sem.at[1, layer, kind],
            device_id=partner, device_id_type=MESH)

    def weight_grads_away(layer):
        trans[0] = dg[...].T
        trans[1] = du[...].T
        trans[2] = hid[...].T
        weight_half(layer, other, gsend, True)

    def weight_grads_here(layer):
        weight_half(layer, me_c, gown, False)

    sides = ((up_d, 1), (down_d, -1))

    def mine(layer, kind, d):
        return gown[layer, kind, d].astype(F32) + grecv[layer, kind, d].astype(F32)

    def first_copy(layer, kind, way):
        columns = slice(way * 256, (way + 1) * 256)
        return pltpu.make_async_remote_copy(
            src_ref=first.at[layer, way, kind],
            dst_ref=ring.at[layer, way, 0, kind, :, columns],
            send_sem=first_sem.at[layer, way, kind], recv_sem=ring_recv.at[layer, way, 0, kind],
            device_id=at_dp(sides[way][0]), device_id_type=MESH)

    def ring_copy(layer, kind, way, step):
        return pltpu.make_async_remote_copy(
            src_ref=ring.at[layer, way, step - 1, kind], dst_ref=ring.at[layer, way, step, kind],
            send_sem=ring_send.at[layer, way, step - 1, kind],
            recv_sem=ring_recv.at[layer, way, step, kind],
            device_id=at_dp(sides[way][0]), device_id_type=MESH)

    def ring_first(layer):
        far = lax.rem(me_d + N_DP // 2, N_DP)

        def step(kind, carry):
            pair_copy(layer, kind).wait()
            value = mine(layer, kind, far).astype(BF)
            for way in range(2):
                first[layer, way, kind] = value[:, way * 256:(way + 1) * 256]
                first_copy(layer, kind, way).start()
            return carry
        lax.fori_loop(0, 3, step, 0)

    def ring_step(layer, number):
        def step(kind, carry):
            for way in range(2):
                target = lax.rem(me_d + N_DP + (4 - number) * sides[way][1], N_DP)
                value = mine(layer, kind, target)
                slot = ring.at[layer, way, number - 1, kind]
                if number == 1:
                    first_copy(layer, kind, way).wait()
                    columns = slice(way * 256, (way + 1) * 256)
                    rest = slice((1 - way) * 256, (2 - way) * 256)
                    slot[:, columns] = (slot[:, columns].astype(F32) + value[:, columns]).astype(BF)
                    slot[:, rest] = value[:, rest].astype(BF)
                else:
                    ring_copy(layer, kind, way, number - 1).wait()
                    slot[...] = (slot[...].astype(F32) + value).astype(BF)
                ring_copy(layer, kind, way, number).start()
            return carry
        lax.fori_loop(0, 3, step, 0)

    def ring_last(layer):
        def step(kind, carry):
            value = mine(layer, kind, me_d)
            for way in range(2):
                ring_copy(layer, kind, way, 3).wait()
                value = value + ring[layer, way, 3, kind].astype(F32)
            gsum[layer, kind] = value.astype(BF)
            return carry
        lax.fori_loop(0, 3, step, 0)

    gather_wait(xr.at[1], both_of_one, 0)
    forward(1)
    hidden_grads(1)
    row_grads(1)
    weight_grads_away(1)
    weight_grads_here(1)
    ring_first(1)
    gather_wait(xr.at[0, 0], inputs_of_zero, 1)
    forward(0)
    to_tokens(1, dy_ref[me_c])
    upd[...] = (gates[0] * dot(picks[0], dxs[1], 1, 0)).astype(BF)
    gather_start(upd, grads_of_zero, 2)
    xd[0, 1, :, my_cols] = upd[...]
    ring_step(1, 1)
    gather_wait(upd, grads_of_zero, 2)
    hidden_grads(0)
    row_grads(0)
    ring_step(1, 2)
    weight_grads_away(0)
    weight_grads_here(0)
    ring_step(1, 3)
    ring_first(0)
    to_tokens(0, dxs[1])
    dx_copy = to_partner(dxs.at[other], dxoth, dx_sem)
    dx_copy.start()
    ring_last(1)
    ring_step(0, 1)
    ring_step(0, 2)
    ring_step(0, 3)
    dx_copy.wait()
    dx_ref[me_c] = dxs[me_c]
    dx_ref[other] = dxoth[...]
    ring_last(0)
    sum_copy = to_partner(gsum.at[other], goth, gs_sem)
    sum_copy.start()
    g_ref[me_c] = gsum[me_c]
    sum_copy.wait()
    g_ref[other] = goth[...]


def backward(saved, dy, pick, gating, weights):
    dma = pltpu.SemaphoreType.DMA
    vmem = pl.BlockSpec(memory_space=pltpu.VMEM)
    scratch = [
        pltpu.VMEM((2, 3, PAD, D), BF),
        pltpu.VMEM((2, ROWS, TOK), BF),
        pltpu.VMEM((2, ROWS, WIDE), F32),
        pltpu.VMEM((3, 2, ROWS, WIDE), BF),
        pltpu.VMEM((2, 2, ROWS, D), BF),
        pltpu.VMEM((ROWS, PAD), F32),
        pltpu.VMEM((ROWS, PAD), F32),
        pltpu.VMEM((ROWS, PAD), BF),
        pltpu.VMEM((ROWS, PAD), BF),
        pltpu.VMEM((ROWS, PAD), BF),
        pltpu.VMEM((3, PAD, ROWS), BF),
        pltpu.VMEM((2, N_TENSOR, ROWS, WIDE), BF),
        pltpu.VMEM((2, N_TENSOR, ROWS, WIDE), BF),
        pltpu.VMEM((2, 3, N_DP, STACK, QUAR), BF),
        pltpu.VMEM((2, 3, N_DP, STACK, QUAR), BF),
        pltpu.VMEM((2, 3, N_DP, STACK, QUAR), BF),
        pltpu.VMEM((2, 2, 3, STACK, QUAR // 2), BF),
        pltpu.VMEM((2, 2, 4, 3, STACK, QUAR), BF),
        pltpu.VMEM((2, 3, STACK, QUAR), BF),
        pltpu.VMEM((3, STACK, QUAR), BF),
        pltpu.VMEM((2, TOK, WIDE), BF),
        pltpu.VMEM((TOK, WIDE), BF),
        pltpu.VMEM((ROWS, WIDE), BF),
        dma((1,)), dma((2,)), dma((2, 2)), dma((2,)),
        dma((3, N_TENSOR)), dma((3, N_TENSOR)), dma((2, N_TENSOR)), dma((2, N_TENSOR)),
        dma((2, 2, 3)), dma((2, 2, 3)), dma((2, 2, 3, 3)), dma((2, 2, 4, 3)), dma((2,)), dma((2,)),
    ]
    return pl.pallas_call(
        kernel,
        out_shape=(
            jax.ShapeDtypeStruct((2, TOK, WIDE), BF),
            jax.ShapeDtypeStruct((2, 3, STACK, QUAR), BF),
        ),
        in_specs=[vmem, vmem, vmem, vmem, pl.BlockSpec(memory_space=pl.ANY)],
        out_specs=(vmem, vmem),
        scratch_shapes=scratch,
        compiler_params=pltpu.CompilerParams(
            collective_id=0, has_side_effects=True, vmem_limit_bytes=60 * 2**20),
        cost_estimate=pl.CostEstimate(
            flops=16 * 2 * ROWS * HID * D, bytes_accessed=30 * 2**20, transcendentals=2 * ROWS * HID),
    )(saved, dy, pick, gating, weights)


def local(x_saved, dy_in, w_all, slot_token, counts, probs, adam_m, adam_v):
    weights = jnp.transpose(w_all[0], (1, 0, 2))
    tokens = jnp.arange(TOK, dtype=jnp.int32)
    pick = (slot_token[0][:, :, None] == tokens).astype(BF)
    positions = jnp.arange(ROWS, dtype=jnp.int32)
    live = positions[None, :] < counts[0]
    gating = jnp.broadcast_to(jnp.where(live, probs[0], 0.0)[:, :, None], (2, ROWS, WIDE))
    results, sums = backward(x_saved[0], dy_in, pick, gating, weights)
    grad_piece = jnp.transpose(sums.reshape(2, 3, 2, PIECE, QUAR), (3, 1, 0, 2, 4)).reshape(-1)
    grad_value = grad_piece.astype(F32)
    moment_one = beta_one * adam_m[0].astype(F32) + (1.0 - beta_one) * grad_value
    moment_two = beta_two * adam_v[0].astype(F32) + (1.0 - beta_two) * grad_value * grad_value
    own = lax.dynamic_slice_in_dim(w_all[0], lax.axis_index("dp") * PIECE, PIECE, 0)
    own_weights = own.reshape(-1).astype(F32)
    update = moment_one / bias_one / (jnp.sqrt(moment_two / bias_two) + adam_epsilon)
    new_weight = own_weights - learning_rate * update
    return (
        results[None],
        grad_piece[None],
        moment_one.astype(BF)[None],
        moment_two.astype(BF)[None],
        new_weight.astype(BF)[None],
    )


def solution(mesh):
    return jax.shard_map(
        local,
        mesh=mesh,
        in_specs=(
            P("segment", None, "dp", "tensor"),
            P(None, "dp", "tensor"),
            P("segment", "tensor", None, None),
            P("segment", None, "dp"),
            P("segment", None, "dp"),
            P("segment", None, "dp"),
            P("segment", ("tensor", "dp")),
            P("segment", ("tensor", "dp")),
        ),
        out_specs=(
            P("segment", None, "dp", "tensor"),
            P("segment", ("tensor", "dp")),
            P("segment", ("tensor", "dp")),
            P("segment", ("tensor", "dp")),
            P("segment", ("tensor", "dp")),
        ),
        check_vma=False,
    )
```

time: 835 us -> 163 us (0.20)
  waiting for transfers between devices: 490 us -> 0 us
  local copies, waits for them, and re-layouts: 160 us -> 7.68 us
  Pallas kernels: 0 us -> 134 us
  other arithmetic: 113 us -> 17.7 us
  matrix products: 31.7 us -> 0 us
  between operations: 16.6 us -> 0.68 us
  starting transfers between devices: 12.8 us -> 0 us
    all_gather x4 -> x0, waiting for transfers between devices: 207 us -> none  [the longest x3 148 us: local(): upstream_full = lax.all_gather(upstream, 'tensor', axis=1, tiled=True)]
    unnamed x10 -> x0, waiting for transfers between devices: 191 us -> none
    pallas_call x0 -> x1, Pallas kernels: none -> 134 us  [backward(): pl.pallas_call(kernel, out_shape=(jax.ShapeDtypeStruct((2, TOK, WIDE), BF...]
    ppermute x5 -> x0, waiting for transfers between devices: 92.3 us -> none  [the longest x3 88.4 us: from_partner(): lax.ppermute(value, axis, [(i, i ^ 1 << apart) for i in range(lax.axis_si...]
    unnamed x36 -> x5, local copies, waits for them, and re-layouts: 38.5 us -> 0.71 us
    dot_general x32 -> x0, matrix products: 31.7 us -> none  [the longest x24 27.9 us: contract(): lax.dot_general(left, right, (((left_dim,), (right_dim,)), ((), ())), pre...]
    convert_element_type x12 -> x3, other arithmetic: 45.7 us -> 17 us  [the longest x1 13.6 us: local(): new_weight.astype(BF)[None]]
    gather x4 -> x0, local copies, waits for them, and re-layouts: 27.6 us -> none  [pick_rows(): return jnp.take(table, positions, axis=0)]
  transfers between devices with their start and end apart: 12 -> 0, of which waited for: 10 -> 0; matrix products, arithmetic and copies ran while one was open for 11% -> 0% of each run, Pallas kernels for 0% -> 0%
where the time goes in v1:
time: 163 us; the launch traced here: 160 us
  Pallas kernels  134 us (82%)
  other arithmetic  17.7 us (11%)
  local copies, waits for them, and re-layouts  7.68 us (5%)
    pallas_call x1, Pallas kernels, backward(): pl.pallas_call(kernel, out_shape=(jax.ShapeDtypeStruct((2, TOK, WIDE), BF...  134 us
    convert_element_type x1, other arithmetic, local(): new_weight.astype(BF)[None]  13.6 us
    convert_element_type x2, local copies, waits for them, and re-layouts, local(): own_weights = own.reshape(-1).astype(F32)  4 us

profile of v1, /device:TPU:2, one launch (start us, length us, event | category | flops | bytes accessed | tf_op | source)
XLA Modules:
  0.0 160.2 jit_solution(14971597895004137635)
XLA Ops:
  0.6 0.8 compare_select_fusion
  1.4 0.8 broadcast_in_dim.9.gate_ref
  2.2 1.6 %fusion.1.pick_ref = bf16[2,256,512]{2,1,0:T(8,128)(2,1)} fusion(s32[2,256]{1,0:T(2,128)} %bitcast.15), kind=kLoop, calls=%fused_computation.6 | loop fusion | flops 524288 | bytes 526336 | tf_op jit(solution)/shard_map/convert_element_type | solution.py:391
  3.9 134.1 %shard_map.119 = (bf16[2,512,128]{2,1,0:T(8,128)(2,1)}, bf16[2,3,112,512]{3,2,1,0:T(8,128)(2,1)}) custom-call(bf16[2,512,128]{2,1,0:T(8,128)(2,1)} %bitcast.17, bf16[2,512,128]{2,1,0:T(8,128)(2,1)} %dy_ref.1, bf16[2,256,512]{2,1,0:T(8,128)(2,1)} %fusion.1.pick_ref, f32[2,256,128]{2,1,0:T(8,128)} %broadcast_in_dim.9.gate_ref, bf16[3,448,2048]{2,1,0:T(8,128)(2,1)} %bitcast.14), custom_call_target="tpu_custom_call" | custom-call | flops 7516192768 | bytes 31457280 | tf_op jit(solution)/shard_map/pallas_call | solution.py:372
  137.9 1.6 %copy.15 = bf16[56,3,2,2,512]{4,3,2,1,0:T(2,128)(2,1)S(1)} copy(bf16[56,3,2,2,512]{4,0,3,1,2:T(8,128)(2,1)} %bitcast.12) | data formatting | bytes 1376256 | tf_op jit(solution)/shard_map/transpose | solution.py:396
  139.6 0.5 broadcast_in_dim_reshape.3
  140.1 0.0 copy-start
  140.1 1.7 %dynamic-slice_convert_fusion = f32[1,56,3,2048]{3,1,2,0:T(8,128)S(1)} fusion(bf16[1,448,3,2048]{3,1,2,0:T(8,128)(2,1)} %param.10, s32[]{:T(128)S(6)} %select_n.12), kind=kLoop, calls=%fused_computation.7 | loop fusion | flops 344064 | bytes 2064388 | tf_op jit(solution)/shard_map/convert_element_type | solution.py:401
  141.9 0.9 copy.16
  142.8 3.1 %reshape.84 = f32[1,344064]{1,0:T(1,128)} reshape(f32[1,56,3,2048]{3,2,1,0:T(4,128)S(1)} %copy.16) | data formatting | bytes 2752512 | tf_op jit(solution)/shard_map/convert_element_type | solution.py:401
  145.9 0.0 copy-done
  145.9 0.0 copy-start.1
  145.9 13.6 %subtract_convert_fusion = (bf16[1,344064]{1,0:T(2,128)(2,1)}, bf16[1,344064]{1,0:T(2,128)(2,1)}, bf16[1,344064]{1,0:T(2,128)(2,1)}) fusion(f32[1,344064]{1,0:T(1,128)} %reshape.84, bf16[1,344064]{1,0:T(2,128)(2,1)S(1)} %broadcast_in_dim_reshape.3, bf16[1,344064]{1,0:T(2,128)(2,1)} %param.14, bf16[1,344064]{1,0:T(2,128)(2,1)} %param.15), kind=kLoop, calls=%fused_computation.2 | loop fusion | flops 6537216 | bytes 5505024 | tf_op jit(solution)/shard_map/convert_element_type | solution.py:409
  159.4 0.0 copy-done.1
  159.5 0.7 copy.18
Async XLA Ops:
  140.1 5.8 %copy-start = (bf16[1,344064]{1,0:T(2,128)(2,1)}, bf16[1,344064]{1,0:T(2,128)(2,1)S(1)}, u32[]{:S(2)}) copy-start(bf16[1,344064]{1,0:T(2,128)(2,1)S(1)} %broadcast_in_dim_reshape.3) | copy-start | bytes 2064388
  145.9 13.6 %copy-start.1 = (bf16[2,512,128]{2,1,0:T(8,128)(2,1)S(1)}, bf16[2,512,128]{2,1,0:T(8,128)(2,1)}, u32[]{:S(2)}) copy-start(bf16[2,512,128]{2,1,0:T(8,128)(2,1)} %get-tuple-element.7) | copy-start | bytes 786436

commit v2 on v1

--- a/solution.py
+++ b/solution.py
@@ -29,6 +29,9 @@
 HALF = D // 2
 QUAR = D // 4
 STACK = 2 * PIECE
+SHARE = 3 * PIECE * D
+CHUNK = 8192
+STEPS = 6
 
 
 def dot(left, right, left_dim, right_dim):
@@ -37,14 +40,16 @@
     )
 
 
-def kernel(x_ref, dy_ref, pick_ref, gate_ref, w_ref, dx_ref, g_ref,
+def kernel(x_ref, dy_ref, slot_ref, count_ref, prob_ref, w_ref,
+           dx_ref, g_ref, w_out_ref,
            w, picks, gates, xr, xd, act, coef, hid, dg, du, trans, back, rs,
            gsend, gown, grecv, first, ring, gsum, goth, dxs, dxoth, upd,
+           flat_g, flat_w, window,
            own_sem, w_sem, pg_sem, xr_sem, ag_send, ag_recv, rs_send, rs_recv,
            gx_sem, first_sem, ring_send, ring_recv, gs_sem, dx_sem):
     me_d, me_t, me_c = lax.axis_index("dp"), lax.axis_index("tensor"), lax.axis_index("segment")
     other = 1 - me_c
-    my_cols = pl.ds(pl.multiple_of(me_t * WIDE, WIDE), WIDE)
+    my_y, my_x = me_t // 4, lax.rem(me_t, 4)
 
     def at_tensor(n):
         return (me_d, n, me_c)
@@ -73,21 +78,25 @@
     for layer in range(2):
         for kind in range(3):
             w[layer, kind, HID:PAD, :] = jnp.zeros((PAD - HID, D), BF)
-    picks[me_c] = pick_ref[me_c]
-    gates[me_c] = gate_ref[me_c]
-
-    def rows_of(micro):
-        choice = pick_ref[micro]
-        picked = dot(choice, x_ref[micro], 1, 0)
-        grads = gate_ref[micro] * dot(choice, dy_ref[micro], 1, 0)
-        return picked.astype(BF), grads.astype(BF)
-
-    there = rows_of(other)
-    xr[2, 0] = there[0]
-    xr[2, 1] = there[1]
-    here = rows_of(me_c)
-    xr[me_c, 0] = here[0]
-    xr[me_c, 1] = here[1]
+    def rows_of(micro, slot):
+        chosen = slot_ref[pl.ds(micro, 1), :]
+        tokens = lax.broadcasted_iota(jnp.int32, (TOK, ROWS), 0)
+        onehot = jnp.where(tokens == chosen, 1.0, 0.0)
+        picks[slot] = onehot.astype(BF)
+        both_counts = count_ref[...]
+        at_micro = lax.broadcasted_iota(jnp.int32, both_counts.shape, 1) == micro
+        count = jnp.sum(jnp.where(at_micro, both_counts, 0), axis=1, keepdims=True)
+        live = lax.broadcasted_iota(jnp.int32, (1, ROWS), 1) < count
+        gating = jnp.where(live, prob_ref[pl.ds(micro, 1), :], 0.0)
+        scale = jnp.broadcast_to(gating, (WIDE, ROWS)).T
+        gates[slot] = scale
+        both = jnp.concatenate([x_ref[micro], dy_ref[micro]], axis=1)
+        picked = dot(picks[slot], both, 0, 0)
+        xr[slot, 0] = picked[:, :WIDE].astype(BF)
+        xr[slot, 1] = (scale * picked[:, WIDE:]).astype(BF)
+
+    rows_of(other, 2)
+    rows_of(me_c, me_c)
 
     pl.semaphore_wait(barrier, N_TENSOR + 2)
 
@@ -102,57 +111,123 @@
     xr_copy.start()
     w_copy = to_partner(w_ref, w.at[me_c, :, pl.ds(0, HID)], w_sem)
     w_copy.start()
-    pick_copy = to_partner(pick_ref.at[other], picks.at[me_c], pg_sem, 0)
+    pick_copy = to_partner(picks.at[2], picks.at[me_c], pg_sem, 0)
     pick_copy.start()
-    gate_copy = to_partner(gate_ref.at[other], gates.at[me_c], pg_sem, 1)
+    gate_copy = to_partner(gates.at[2], gates.at[me_c], pg_sem, 1)
     gate_copy.start()
 
-    def gather_copy(src, dst, use, n, owner):
-        columns = pl.ds(pl.multiple_of(owner * WIDE, WIDE), WIDE)
+    def hop(use, phase, which, ref, device):
         return pltpu.make_async_remote_copy(
-            src_ref=src, dst_ref=dst(columns), send_sem=ag_send.at[use, n],
-            recv_sem=ag_recv.at[use, owner], device_id=at_tensor(n), device_id_type=MESH)
-
-    def gather_start(src, dst, use):
-        def step(k, carry):
-            gather_copy(src, dst, use, peer(k), me_t).start()
-            return carry
-        lax.fori_loop(1, N_TENSOR, step, 0)
-
-    def gather_wait(src, dst, use):
-        def step(k, carry):
-            n = peer(k)
-            gather_copy(src, dst, use, n, n).wait_recv()
-            gather_copy(src, dst, use, n, me_t).wait_send()
-            return carry
-        lax.fori_loop(1, N_TENSOR, step, 0)
-
-    def both_of_one(columns):
-        return xd.at[1, :, :, columns]
-
-    def inputs_of_zero(columns):
-        return xd.at[0, 0, :, columns]
-
-    def grads_of_zero(columns):
-        return xd.at[0, 1, :, columns]
+            src_ref=ref, dst_ref=ref, send_sem=ag_send.at[use, phase, which],
+            recv_sem=ag_recv.at[use, phase, which], device_id=device, device_id_type=MESH)
+
+    class Piece:
+        def __init__(self, use, layer, kind, start, rows, x_first, direct):
+            self.use, self.layer, self.kind = use, layer, kind
+            self.start, self.rows, self.x_first, self.direct = start, rows, x_first, direct
+
+        def at(self, phase, shift):
+            if self.x_first == (phase == 0):
+                return at_tensor(my_y * 4 + (my_x + shift) % 4)
+            return at_tensor((my_y + shift) % 4 * 4 + my_x)
+
+        def block(self, phase, shift, part):
+            along_x = self.x_first == (phase == 0)
+            low, count = {"all": (0, self.rows), "low": (0, self.rows // 2),
+                          "high": (self.rows // 2, self.rows // 2)}[part]
+            rows = slice(self.start + low, self.start + low + count)
+            index = ((my_x if along_x else my_y) + shift) % 4
+            columns = pl.ds(pl.multiple_of((index if along_x else my_x) * WIDE, WIDE), WIDE)
+            array = xd.at[self.layer] if self.kind is None else xd.at[self.layer, pl.ds(self.kind, 1)]
+            if phase == 0:
+                return array.at[:, my_y if along_x else index, rows, columns]
+            return array.at[:, :, rows, columns] if along_x else array.at[:, index, rows, :]
+
+        def put(self, values):
+            columns = pl.ds(pl.multiple_of(my_x * WIDE, WIDE), WIDE)
+            first = 0 if self.kind is None else self.kind
+            for index, value in enumerate(values):
+                rows = slice(self.start, self.start + self.rows)
+                xd[self.layer, first + index, my_y, rows, columns] = value[rows]
+
+        def hops(self, phase):
+            own = [(0, 1, "all", 0, 3), (1, 3, "all", 0, 1)]
+            if self.direct:
+                return own + [(2, 2, "all", 0, 2)], []
+            return own, [(2, 1, "low", 3, 2), (3, 3, "high", 1, 2)]
+
+        def copy(self, phase, hop_of, owner):
+            which, shift, part, _, _ = hop_of
+            return hop(self.use, phase, which, self.block(phase, owner, part), self.at(phase, shift))
+
+        def send(self, phase):
+            if phase == 1:
+                self.finish(0)
+            for one in self.hops(phase)[0]:
+                self.copy(phase, one, one[3]).start()
+
+        def forward(self, phase):
+            own, later = self.hops(phase)
+            for one, two in zip(own, later):
+                self.copy(phase, one, one[4]).wait_recv()
+                self.copy(phase, two, two[3]).start()
+
+        def finish(self, phase):
+            own, later = self.hops(phase)
+            for one in later or own:
+                self.copy(phase, one, one[4]).wait_recv()
+
+        def drain(self):
+            for phase in range(2):
+                own, later = self.hops(phase)
+                for one in own + later:
+                    self.copy(phase, one, one[3]).wait_send()
+
+    part = ROWS // 2
+
+    def pieces_of(use, layer, kind, direct):
+        return (Piece(use, layer, kind, 0, part, True, direct),
+                Piece(use + 1, layer, kind, part, part, False, direct))
+
+    ones = pieces_of(0, 1, None, True)
+    zeros = pieces_of(2, 0, 0, True)
+    grads = pieces_of(4, 0, 1, True)
+
+    def launch(pieces, values):
+        for piece in pieces:
+            piece.put(values)
+            piece.send(0)
 
     xr_copy.wait()
-    gather_start(xr.at[1], both_of_one, 0)
-    gather_start(xr.at[0, 0], inputs_of_zero, 1)
-    for kind in range(2):
-        xd[1, kind, :, my_cols] = xr[1, kind]
-    xd[0, 0, :, my_cols] = xr[0, 0]
+    launch(ones, (xr[1, 0], xr[1, 1]))
+    for piece in ones:
+        piece.forward(0)
+    for piece in ones:
+        piece.send(1)
+    launch(zeros, (xr[0, 0],))
+    for piece in ones:
+        piece.forward(1)
+    for piece in zeros:
+        piece.forward(0)
+    for piece in zeros:
+        piece.send(1)
     own_w.wait()
     w_copy.wait()
     pick_copy.wait()
     gate_copy.wait()
 
+    def wide_dot(layer, kind, matrix, span):
+        total = None
+        for y in range(4):
+            part = dot(xd[layer, kind, y], w[layer, matrix, span, y * QUAR:(y + 1) * QUAR], 1, 1)
+            total = part if total is None else total + part
+        return total
+
     def forward(layer):
         def step(block, carry):
             span = pl.ds(pl.multiple_of(block * 256, 256), 256)
-            inputs = xd[layer, 0]
-            gate_pre = dot(inputs, w[layer, 0, span, :], 1, 1)
-            up_pre = dot(inputs, w[layer, 1, span, :], 1, 1)
+            gate_pre = wide_dot(layer, 0, 0, span)
+            up_pre = wide_dot(layer, 0, 1, span)
             sig = 1.0 / (1.0 + jnp.exp(-gate_pre))
             active = gate_pre * sig
             act[:, span] = active
@@ -164,7 +239,7 @@
     def hidden_grads(layer):
         def step(block, carry):
             span = pl.ds(pl.multiple_of(block * 256, 256), 256)
-            grad = dot(xd[layer, 1], w[layer, 2, span, :], 1, 1)
+            grad = wide_dot(layer, 1, 2, span)
             dg[:, span] = (grad * coef[:, span]).astype(BF)
             du[:, span] = (grad * act[:, span]).astype(BF)
             return carry
@@ -204,15 +279,14 @@
         total = summed_rows(layer)
         high = total.astype(BF)
         low = (total - high.astype(F32)).astype(BF)
-        spread = dot(picks[layer], high, 0, 0) + dot(picks[layer], low, 0, 0)
+        spread = dot(picks[layer], high, 1, 0) + dot(picks[layer], low, 1, 0)
         dxs[layer] = (upstream.astype(F32) + spread).astype(BF)
 
     def weight_half(layer, half, dst, send):
         def step(kind, carry):
             parts = []
             for quarter in range(2):
-                span = pl.ds(pl.multiple_of(half * HALF + quarter * QUAR, QUAR), QUAR)
-                parts.append(dot(trans[kind], xd[layer, kind // 2, :, span], 1, 0))
+                parts.append(dot(trans[kind], xd[layer, kind // 2, half * 2 + quarter], 1, 0))
             for d in range(N_DP):
                 rows = slice(d * PIECE, (d + 1) * PIECE)
                 both = jnp.concatenate([parts[0][rows], parts[1][rows]], axis=0)
@@ -298,55 +372,81 @@
             return carry
         lax.fori_loop(0, 3, step, 0)
 
-    gather_wait(xr.at[1], both_of_one, 0)
+    def flat_weights():
+        first_row = me_d * PIECE
+        offset = lax.rem(first_row, 16)
+        rows = pl.ds(pl.multiple_of(first_row - offset, 16), 64)
+        for kind in range(3):
+            window[...] = w[me_c, kind, rows, :].astype(F32)
+            for block in range(16):
+                flat_w[pl.ds(kind * 16 + block, PIECE, stride=48), :] = window[
+                    pl.ds(pl.multiple_of(offset, 8), PIECE), block * WIDE:(block + 1) * WIDE]
+
+    def flat_sums(source, half):
+        for kind in range(3):
+            for block in range(8):
+                quarter, columns = block // 4, slice(block % 4 * WIDE, (block % 4 + 1) * WIDE)
+                value = source[kind, quarter * PIECE:(quarter + 1) * PIECE, columns]
+                flat_g[pl.ds(half * 8 + kind * 16 + block, PIECE, stride=48), :] = value.astype(F32)
+
+    for piece in ones:
+        piece.finish(1)
     forward(1)
     hidden_grads(1)
+    weight_grads_away(1)
     row_grads(1)
-    weight_grads_away(1)
     weight_grads_here(1)
     ring_first(1)
-    gather_wait(xr.at[0, 0], inputs_of_zero, 1)
+    for piece in zeros:
+        piece.finish(1)
     forward(0)
     to_tokens(1, dy_ref[me_c])
-    upd[...] = (gates[0] * dot(picks[0], dxs[1], 1, 0)).astype(BF)
-    gather_start(upd, grads_of_zero, 2)
-    xd[0, 1, :, my_cols] = upd[...]
+    upd[...] = (gates[0] * dot(picks[0], dxs[1], 0, 0)).astype(BF)
+    launch(grads, (upd[...],))
     ring_step(1, 1)
-    gather_wait(upd, grads_of_zero, 2)
+    for piece in grads:
+        piece.send(1)
+    flat_weights()
+    ring_step(1, 2)
+    for piece in grads:
+        piece.finish(1)
     hidden_grads(0)
-    row_grads(0)
-    ring_step(1, 2)
     weight_grads_away(0)
     weight_grads_here(0)
+    row_grads(0)
     ring_step(1, 3)
     ring_first(0)
+    ring_step(0, 1)
+    ring_last(1)
+    ring_step(0, 2)
     to_tokens(0, dxs[1])
     dx_copy = to_partner(dxs.at[other], dxoth, dx_sem)
     dx_copy.start()
-    ring_last(1)
-    ring_step(0, 1)
-    ring_step(0, 2)
     ring_step(0, 3)
+    for piece in ones + zeros + grads:
+        piece.drain()
     dx_copy.wait()
     dx_ref[me_c] = dxs[me_c]
     dx_ref[other] = dxoth[...]
     ring_last(0)
     sum_copy = to_partner(gsum.at[other], goth, gs_sem)
     sum_copy.start()
-    g_ref[me_c] = gsum[me_c]
+    flat_sums(gsum.at[me_c], me_c)
     sum_copy.wait()
-    g_ref[other] = goth[...]
-
-
-def backward(saved, dy, pick, gating, weights):
+    flat_sums(goth, other)
+    g_ref[...] = flat_g[...].astype(BF)
+    w_out_ref[...] = flat_w[...].astype(BF)
+
+
+def backward(saved, dy, slots, counts, probs, weights):
     dma = pltpu.SemaphoreType.DMA
-    vmem = pl.BlockSpec(memory_space=pltpu.VMEM)
+    vmem, hbm = pl.BlockSpec(memory_space=pltpu.VMEM), pl.BlockSpec(memory_space=pl.ANY)
     scratch = [
         pltpu.VMEM((2, 3, PAD, D), BF),
-        pltpu.VMEM((2, ROWS, TOK), BF),
-        pltpu.VMEM((2, ROWS, WIDE), F32),
+        pltpu.VMEM((3, TOK, ROWS), BF),
+        pltpu.VMEM((3, ROWS, WIDE), F32),
         pltpu.VMEM((3, 2, ROWS, WIDE), BF),
-        pltpu.VMEM((2, 2, ROWS, D), BF),
+        pltpu.VMEM((2, 2, 4, ROWS, QUAR), BF),
         pltpu.VMEM((ROWS, PAD), F32),
         pltpu.VMEM((ROWS, PAD), F32),
         pltpu.VMEM((ROWS, PAD), BF),
@@ -365,49 +465,71 @@
         pltpu.VMEM((2, TOK, WIDE), BF),
         pltpu.VMEM((TOK, WIDE), BF),
         pltpu.VMEM((ROWS, WIDE), BF),
+        pltpu.VMEM((SHARE // WIDE, WIDE), F32),
+        pltpu.VMEM((SHARE // WIDE, WIDE), F32),
+        pltpu.VMEM((64, D), F32),
         dma((1,)), dma((2,)), dma((2, 2)), dma((2,)),
-        dma((3, N_TENSOR)), dma((3, N_TENSOR)), dma((2, N_TENSOR)), dma((2, N_TENSOR)),
+        dma((6, 2, 4)), dma((6, 2, 4)), dma((2, N_TENSOR)), dma((2, N_TENSOR)),
         dma((2, 2, 3)), dma((2, 2, 3)), dma((2, 2, 3, 3)), dma((2, 2, 4, 3)), dma((2,)), dma((2,)),
     ]
     return pl.pallas_call(
         kernel,
-        out_shape=(
-            jax.ShapeDtypeStruct((2, TOK, WIDE), BF),
-            jax.ShapeDtypeStruct((2, 3, STACK, QUAR), BF),
-        ),
-        in_specs=[vmem, vmem, vmem, vmem, pl.BlockSpec(memory_space=pl.ANY)],
-        out_specs=(vmem, vmem),
+        out_shape=(jax.ShapeDtypeStruct((2, TOK, WIDE), BF),)
+        + (jax.ShapeDtypeStruct((SHARE // WIDE, WIDE), BF),) * 2,
+        in_specs=[vmem] * 5 + [hbm],
+        out_specs=(vmem,) * 3,
         scratch_shapes=scratch,
         compiler_params=pltpu.CompilerParams(
             collective_id=0, has_side_effects=True, vmem_limit_bytes=60 * 2**20),
         cost_estimate=pl.CostEstimate(
             flops=16 * 2 * ROWS * HID * D, bytes_accessed=30 * 2**20, transcendentals=2 * ROWS * HID),
-    )(saved, dy, pick, gating, weights)
+    )(saved, dy, slots, counts, probs, weights)
+
+
+def finish(dx_ref, g_ref, w_ref, m_ref, v_ref, dx_out, sum_out, m_out, v_out, w_out):
+    @pl.when(pl.program_id(0) == 0)
+    def _():
+        dx_out[...] = dx_ref[...]
+
+    def step(index, carry):
+        span = pl.ds(pl.multiple_of(index * CHUNK, CHUNK), CHUNK)
+        lines = CHUNK // WIDE
+        rows = pl.ds(pl.multiple_of(index * lines, lines), lines)
+        grad = g_ref[rows, :].astype(F32)
+        moment_one = m_ref[:, span].reshape(lines, WIDE).astype(F32)
+        moment_two = v_ref[:, span].reshape(lines, WIDE).astype(F32)
+        moment_one = beta_one * moment_one + (1.0 - beta_one) * grad
+        moment_two = beta_two * moment_two + (1.0 - beta_two) * grad * grad
+        update = moment_one / bias_one / (jnp.sqrt(moment_two / bias_two) + adam_epsilon)
+        fresh = w_ref[rows, :].astype(F32) - learning_rate * update
+        sum_out[:, span] = grad.astype(BF).reshape(1, CHUNK)
+        m_out[:, span] = moment_one.astype(BF).reshape(1, CHUNK)
+        v_out[:, span] = moment_two.astype(BF).reshape(1, CHUNK)
+        w_out[:, span] = fresh.astype(BF).reshape(1, CHUNK)
+        return carry
+    lax.fori_loop(0, SHARE // STEPS // CHUNK, step, 0, unroll=True)
+
+
+def adam(dx, grad, weights, adam_m, adam_v):
+    block = SHARE // STEPS
+    whole = pl.BlockSpec((2, TOK, WIDE), lambda i: (0, 0, 0))
+    lines = pl.BlockSpec((block // WIDE, WIDE), lambda i: (i, 0))
+    flat = pl.BlockSpec((1, block), lambda i: (0, i))
+    return pl.pallas_call(
+        finish,
+        out_shape=(jax.ShapeDtypeStruct(dx.shape, BF),) + (jax.ShapeDtypeStruct((1, SHARE), BF),) * 4,
+        grid=(STEPS,),
+        in_specs=[whole, lines, lines, flat, flat],
+        out_specs=(whole,) + (flat,) * 4,
+        compiler_params=pltpu.CompilerParams(vmem_limit_bytes=60 * 2**20),
+    )(dx, grad, weights, adam_m, adam_v)
 
 
 def local(x_saved, dy_in, w_all, slot_token, counts, probs, adam_m, adam_v):
     weights = jnp.transpose(w_all[0], (1, 0, 2))
-    tokens = jnp.arange(TOK, dtype=jnp.int32)
-    pick = (slot_token[0][:, :, None] == tokens).astype(BF)
-    positions = jnp.arange(ROWS, dtype=jnp.int32)
-    live = positions[None, :] < counts[0]
-    gating = jnp.broadcast_to(jnp.where(live, probs[0], 0.0)[:, :, None], (2, ROWS, WIDE))
-    results, sums = backward(x_saved[0], dy_in, pick, gating, weights)
-    grad_piece = jnp.transpose(sums.reshape(2, 3, 2, PIECE, QUAR), (3, 1, 0, 2, 4)).reshape(-1)
-    grad_value = grad_piece.astype(F32)
-    moment_one = beta_one * adam_m[0].astype(F32) + (1.0 - beta_one) * grad_value
-    moment_two = beta_two * adam_v[0].astype(F32) + (1.0 - beta_two) * grad_value * grad_value
-    own = lax.dynamic_slice_in_dim(w_all[0], lax.axis_index("dp") * PIECE, PIECE, 0)
-    own_weights = own.reshape(-1).astype(F32)
-    update = moment_one / bias_one / (jnp.sqrt(moment_two / bias_two) + adam_epsilon)
-    new_weight = own_weights - learning_rate * update
-    return (
-        results[None],
-        grad_piece[None],
-        moment_one.astype(BF)[None],
-        moment_two.astype(BF)[None],
-        new_weight.astype(BF)[None],
-    )
+    results, grad, own = backward(x_saved[0], dy_in, slot_token[0], counts[0].T, probs[0], weights)
+    results, sums, new_m, new_v, new_w = adam(results, grad, own, adam_m, adam_v)
+    return (results[None], sums, new_m, new_v, new_w)
 
 
 def solution(mesh):

time: 163 us -> 121 us (0.74)
  other arithmetic: 17.7 us -> 0 us
  Pallas kernels: 134 us -> 118 us
  local copies, waits for them, and re-layouts: 7.68 us -> 0 us
    pallas_call x1, Pallas kernels: 134 us -> 111 us  [backward(): pl.pallas_call(kernel, out_shape=(jax.ShapeDtypeStruct((2, TOK, WIDE), BF...]
    convert_element_type x3 -> x0, other arithmetic: 17 us -> none  [the longest x1 13.6 us: local(): new_weight.astype(BF)[None]]
    pallas_call x0 -> x1, Pallas kernels: none -> 6.86 us  [adam(): pl.pallas_call(finish, out_shape=(jax.ShapeDtypeStruct(dx.shape, BF),) +...]
    convert_element_type x2 -> x0, local copies, waits for them, and re-layouts: 4 us -> none  [local(): own_weights = own.reshape(-1).astype(F32)]
    transpose x1 -> x0, local copies, waits for them, and re-layouts: 1.63 us -> none  [local(): jnp.transpose(sums.reshape(2, 3, 2, PIECE, QUAR), (3, 1, 0, 2, 4))]
where the time goes in v2:
time: 121 us; the launch traced here: 119 us
  Pallas kernels  118 us (98%)
    pallas_call x1, Pallas kernels, backward(): pl.pallas_call(kernel, out_shape=(jax.ShapeDtypeStruct((2, TOK, WIDE), BF...  111 us
    pallas_call x1, Pallas kernels, adam(): pl.pallas_call(finish, out_shape=(jax.ShapeDtypeStruct(dx.shape, BF),) +...  6.86 us

profile of v2, /device:TPU:2, one launch (start us, length us, event | category | flops | bytes accessed | tf_op | source)
XLA Modules:
  0.0 118.8 jit_solution(599070773437106788)
XLA Ops:
  0.6 111.3 %shard_map.119 = (bf16[2,512,128]{2,1,0:T(8,128)(2,1)}, bf16[2688,128]{1,0:T(8,128)(2,1)}, bf16[2688,128]{1,0:T(8,128)(2,1)}) custom-call(bf16[2,512,128]{2,1,0:T(8,128)(2,1)} %bitcast.9, bf16[2,512,128]{2,1,0:T(8,128)(2,1)} %dy_ref.1, s32[2,256]{1,0:T(2,128)} %bitcast.11, s32[1,2]{1,0:T(1,128)} %bitcast.13, f32[2,256]{1,0:T(2,128)} %bitcast.12, ...), custom_call_target="tpu_custom_call" | custom-call | flops 7516192768 | bytes 31457280 | tf_op jit(solution)/shard_map/pallas_call | solution.py:475
  111.9 6.9 %shard_map.120 = (bf16[2,512,128]{2,1,0:T(8,128)(2,1)}, bf16[1,344064]{1,0:T(2,128)(2,1)}, bf16[1,344064]{1,0:T(2,128)(2,1)}, bf16[1,344064]{1,0:T(2,128)(2,1)}, bf16[1,344064]{1,0:T(2,128)(2,1)}) custom-call(bf16[2,512,128]{2,1,0:T(8,128)(2,1)} %get-tuple-element.13.dx_ref, bf16[2688,128]{1,0:T(8,128)(2,1)} %get-tuple-element.14.g_ref, ...), custom_call_target="tpu_custom_call" | custom-call | tf_op jit(solution)/shard_map/pallas_call | solution.py:518

commit v3 on v2

--- a/solution.py
+++ b/solution.py
@@ -40,13 +40,13 @@
     )
 
 
-def kernel(x_ref, dy_ref, slot_ref, count_ref, prob_ref, w_ref,
-           dx_ref, g_ref, w_out_ref,
-           w, picks, gates, xr, xd, act, coef, hid, dg, du, trans, back, rs,
-           gsend, gown, grecv, first, ring, gsum, goth, dxs, dxoth, upd,
-           flat_g, flat_w, window,
+def kernel(x_hbm, dy_hbm, slot_ref, count_ref, prob_ref, w_ref,
+           dx_hbm, g_hbm, w_hbm,
+           x_ref, dy_ref, dx_ref, g_ref, w_out_ref, w, picks, gates, xr, xd, act, coef, hid, dg, du, trans, back, rs,
+           gsend, gown, grecv, first, ring, fin, dxs, dxoth, upd,
+           flat_g, flat_w, window, owned, away,
            own_sem, w_sem, pg_sem, xr_sem, ag_send, ag_recv, rs_send, rs_recv,
-           gx_sem, first_sem, ring_send, ring_recv, gs_sem, dx_sem):
+           gx_sem, first_sem, ring_send, ring_recv, part_sem, dx_sem, fin_sem, in_sem, out_sem):
     me_d, me_t, me_c = lax.axis_index("dp"), lax.axis_index("tensor"), lax.axis_index("segment")
     other = 1 - me_c
     my_y, my_x = me_t // 4, lax.rem(me_t, 4)
@@ -62,6 +62,11 @@
 
     def peer(k):
         return ((me_t // 4 + k // 4) % 4) * 4 + (me_t % 4 + k % 4) % 4
+
+    saved_in = pltpu.make_async_copy(x_hbm, x_ref, in_sem.at[0])
+    grads_in = pltpu.make_async_copy(dy_hbm, dy_ref, in_sem.at[1])
+    saved_in.start()
+    grads_in.start()
 
     barrier = pltpu.get_barrier_semaphore()
 
@@ -70,8 +75,9 @@
         return carry
     lax.fori_loop(1, N_TENSOR, greet, 0)
     pl.semaphore_signal(barrier, inc=1, device_id=partner, device_id_type=MESH)
-    pl.semaphore_signal(barrier, inc=1, device_id=at_dp(up_d), device_id_type=MESH)
-    pl.semaphore_signal(barrier, inc=1, device_id=at_dp(down_d), device_id_type=MESH)
+    for layer in range(2):
+        pl.semaphore_signal(barrier, inc=1, device_id=(up_d, me_t, layer), device_id_type=MESH)
+        pl.semaphore_signal(barrier, inc=1, device_id=(down_d, me_t, layer), device_id_type=MESH)
 
     own_w = pltpu.make_async_copy(w_ref, w.at[me_c, :, pl.ds(0, HID)], own_sem.at[0])
     own_w.start()
@@ -95,10 +101,12 @@
         xr[slot, 0] = picked[:, :WIDE].astype(BF)
         xr[slot, 1] = (scale * picked[:, WIDE:]).astype(BF)
 
+    saved_in.wait()
+    grads_in.wait()
     rows_of(other, 2)
     rows_of(me_c, me_c)
 
-    pl.semaphore_wait(barrier, N_TENSOR + 2)
+    pl.semaphore_wait(barrier, N_TENSOR + 4)
 
     def to_partner(src, dst, sems, index=None):
         send = sems.at[0] if index is None else sems.at[0, index]
@@ -358,19 +366,23 @@
                 else:
                     ring_copy(layer, kind, way, number - 1).wait()
                     slot[...] = (slot[...].astype(F32) + value).astype(BF)
-                ring_copy(layer, kind, way, number).start()
+                if number < 3:
+                    ring_copy(layer, kind, way, number).start()
+                else:
+                    last_copy(layer, kind, way, me_c).start()
             return carry
         lax.fori_loop(0, 3, step, 0)
 
-    def ring_last(layer):
-        def step(kind, carry):
-            value = mine(layer, kind, me_d)
-            for way in range(2):
-                ring_copy(layer, kind, way, 3).wait()
-                value = value + ring[layer, way, 3, kind].astype(F32)
-            gsum[layer, kind] = value.astype(BF)
-            return carry
-        lax.fori_loop(0, 3, step, 0)
+    def last_copy(layer, kind, way, half):
+        return pltpu.make_async_remote_copy(
+            src_ref=ring.at[layer, way, 2, kind], dst_ref=fin.at[half, way, kind],
+            send_sem=ring_send.at[layer, way, 2, kind], recv_sem=fin_sem.at[half, way, kind],
+            device_id=(sides[way][0], me_t, layer), device_id_type=MESH)
+
+    def own_parts():
+        for kind in range(3):
+            owned[me_c, kind] = mine(me_c, kind, me_d).astype(BF)
+            away[kind] = mine(other, kind, me_d).astype(BF)
 
     def flat_weights():
         first_row = me_d * PIECE
@@ -382,42 +394,49 @@
                 flat_w[pl.ds(kind * 16 + block, PIECE, stride=48), :] = window[
                     pl.ds(pl.multiple_of(offset, 8), PIECE), block * WIDE:(block + 1) * WIDE]
 
-    def flat_sums(source, half):
+    def flat_sums():
         for kind in range(3):
-            for block in range(8):
-                quarter, columns = block // 4, slice(block % 4 * WIDE, (block % 4 + 1) * WIDE)
-                value = source[kind, quarter * PIECE:(quarter + 1) * PIECE, columns]
-                flat_g[pl.ds(half * 8 + kind * 16 + block, PIECE, stride=48), :] = value.astype(F32)
+            for half in range(2):
+                value = owned[half, kind].astype(F32)
+                for way in range(2):
+                    last_copy(0, kind, way, half).wait_recv()
+                    value = value + fin[half, way, kind].astype(F32)
+                for block in range(8):
+                    rows = slice(block // 4 * PIECE, (block // 4 + 1) * PIECE)
+                    columns = slice(block % 4 * WIDE, (block % 4 + 1) * WIDE)
+                    flat_g[pl.ds(half * 8 + kind * 16 + block, PIECE, stride=48), :] = value[rows, columns]
 
     for piece in ones:
         piece.finish(1)
     forward(1)
     hidden_grads(1)
+    row_grads(1)
     weight_grads_away(1)
-    row_grads(1)
     weight_grads_here(1)
     ring_first(1)
+    ring_step(1, 1)
     for piece in zeros:
         piece.finish(1)
     forward(0)
     to_tokens(1, dy_ref[me_c])
     upd[...] = (gates[0] * dot(picks[0], dxs[1], 0, 0)).astype(BF)
     launch(grads, (upd[...],))
-    ring_step(1, 1)
+    ring_step(1, 2)
     for piece in grads:
         piece.send(1)
     flat_weights()
-    ring_step(1, 2)
     for piece in grads:
         piece.finish(1)
+    ring_step(1, 3)
     hidden_grads(0)
     weight_grads_away(0)
     weight_grads_here(0)
     row_grads(0)
-    ring_step(1, 3)
     ring_first(0)
+    own_parts()
+    part_copy = to_partner(away, owned.at[me_c], part_sem)
+    part_copy.start()
     ring_step(0, 1)
-    ring_last(1)
     ring_step(0, 2)
     to_tokens(0, dxs[1])
     dx_copy = to_partner(dxs.at[other], dxoth, dx_sem)
@@ -425,23 +444,37 @@
     ring_step(0, 3)
     for piece in ones + zeros + grads:
         piece.drain()
+    w_out_ref[...] = flat_w[...].astype(BF)
+    own_out = pltpu.make_async_copy(w_out_ref, w_hbm, out_sem.at[0])
+    own_out.start()
     dx_copy.wait()
     dx_ref[me_c] = dxs[me_c]
     dx_ref[other] = dxoth[...]
-    ring_last(0)
-    sum_copy = to_partner(gsum.at[other], goth, gs_sem)
-    sum_copy.start()
-    flat_sums(gsum.at[me_c], me_c)
-    sum_copy.wait()
-    flat_sums(goth, other)
+    dx_out = pltpu.make_async_copy(dx_ref, dx_hbm, out_sem.at[1])
+    dx_out.start()
+    part_copy.wait()
+    flat_sums()
     g_ref[...] = flat_g[...].astype(BF)
-    w_out_ref[...] = flat_w[...].astype(BF)
+    g_out = pltpu.make_async_copy(g_ref, g_hbm, out_sem.at[2])
+    g_out.start()
+    for layer in range(2):
+        for kind in range(3):
+            for way in range(2):
+                last_copy(layer, kind, way, me_c).wait_send()
+    own_out.wait()
+    dx_out.wait()
+    g_out.wait()
 
 
 def backward(saved, dy, slots, counts, probs, weights):
     dma = pltpu.SemaphoreType.DMA
     vmem, hbm = pl.BlockSpec(memory_space=pltpu.VMEM), pl.BlockSpec(memory_space=pl.ANY)
     scratch = [
+        pltpu.VMEM((2, TOK, WIDE), BF),
+        pltpu.VMEM((2, TOK, WIDE), BF),
+        pltpu.VMEM((2, TOK, WIDE), BF),
+        pltpu.VMEM((SHARE // WIDE, WIDE), BF),
+        pltpu.VMEM((SHARE // WIDE, WIDE), BF),
         pltpu.VMEM((2, 3, PAD, D), BF),
         pltpu.VMEM((3, TOK, ROWS), BF),
         pltpu.VMEM((3, ROWS, WIDE), F32),
@@ -459,25 +492,27 @@
         pltpu.VMEM((2, 3, N_DP, STACK, QUAR), BF),
         pltpu.VMEM((2, 3, N_DP, STACK, QUAR), BF),
         pltpu.VMEM((2, 2, 3, STACK, QUAR // 2), BF),
-        pltpu.VMEM((2, 2, 4, 3, STACK, QUAR), BF),
-        pltpu.VMEM((2, 3, STACK, QUAR), BF),
-        pltpu.VMEM((3, STACK, QUAR), BF),
+        pltpu.VMEM((2, 2, 3, 3, STACK, QUAR), BF),
+        pltpu.VMEM((2, 2, 3, STACK, QUAR), BF),
         pltpu.VMEM((2, TOK, WIDE), BF),
         pltpu.VMEM((TOK, WIDE), BF),
         pltpu.VMEM((ROWS, WIDE), BF),
         pltpu.VMEM((SHARE // WIDE, WIDE), F32),
         pltpu.VMEM((SHARE // WIDE, WIDE), F32),
         pltpu.VMEM((64, D), F32),
+        pltpu.VMEM((2, 3, STACK, QUAR), BF),
+        pltpu.VMEM((3, STACK, QUAR), BF),
         dma((1,)), dma((2,)), dma((2, 2)), dma((2,)),
         dma((6, 2, 4)), dma((6, 2, 4)), dma((2, N_TENSOR)), dma((2, N_TENSOR)),
-        dma((2, 2, 3)), dma((2, 2, 3)), dma((2, 2, 3, 3)), dma((2, 2, 4, 3)), dma((2,)), dma((2,)),
+        dma((2, 2, 3)), dma((2, 2, 3)), dma((2, 2, 3, 3)), dma((2, 2, 3, 3)), dma((2,)), dma((2,)),
+        dma((2, 2, 3)), dma((2,)), dma((3,)),
     ]
     return pl.pallas_call(
         kernel,
         out_shape=(jax.ShapeDtypeStruct((2, TOK, WIDE), BF),)
         + (jax.ShapeDtypeStruct((SHARE // WIDE, WIDE), BF),) * 2,
-        in_specs=[vmem] * 5 + [hbm],
-        out_specs=(vmem,) * 3,
+        in_specs=[hbm, hbm, vmem, vmem, vmem, hbm],
+        out_specs=(hbm,) * 3,
         scratch_shapes=scratch,
         compiler_params=pltpu.CompilerParams(
             collective_id=0, has_side_effects=True, vmem_limit_bytes=60 * 2**20),

time: 121 us -> 109 us (0.901); the launches traced: 119 us -> 109 us
  Pallas kernels: 118 us -> 108 us
    pallas_call x1, Pallas kernels: 111 us -> 101 us  [backward(): pl.pallas_call(kernel, out_shape=(jax.ShapeDtypeStruct((2, TOK, WIDE), BF...]
where the time goes in v3:
time: 109 us
  Pallas kernels  108 us (99%)
    pallas_call x1, Pallas kernels, backward(): pl.pallas_call(kernel, out_shape=(jax.ShapeDtypeStruct((2, TOK, WIDE), BF...  101 us
    pallas_call x1, Pallas kernels, adam(): pl.pallas_call(finish, out_shape=(jax.ShapeDtypeStruct(dx.shape, BF),) +...  6.86 us

profile of v3, /device:TPU:2, one launch (start us, length us, event | category | flops | bytes accessed | tf_op | source)
XLA Modules:
  0.0 108.9 jit_solution(18318017507120011182)
XLA Ops:
  0.6 101.4 %shard_map.119 = (bf16[2,512,128]{2,1,0:T(8,128)(2,1)}, bf16[2688,128]{1,0:T(8,128)(2,1)}, bf16[2688,128]{1,0:T(8,128)(2,1)}) custom-call(bf16[2,512,128]{2,1,0:T(8,128)(2,1)} %bitcast.9, bf16[2,512,128]{2,1,0:T(8,128)(2,1)} %dy_hbm.1, s32[2,256]{1,0:T(2,128)} %bitcast.11, s32[1,2]{1,0:T(1,128)} %bitcast.13, f32[2,256]{1,0:T(2,128)} %bitcast.12, ...), custom_call_target="tpu_custom_call" | custom-call | flops 7516192768 | bytes 31457280 | tf_op jit(solution)/shard_map/pallas_call | solution.py:510
  102.0 6.9 %shard_map.120 = (bf16[2,512,128]{2,1,0:T(8,128)(2,1)}, bf16[1,344064]{1,0:T(2,128)(2,1)}, bf16[1,344064]{1,0:T(2,128)(2,1)}, bf16[1,344064]{1,0:T(2,128)(2,1)}, bf16[1,344064]{1,0:T(2,128)(2,1)}) custom-call(bf16[2,512,128]{2,1,0:T(8,128)(2,1)} %get-tuple-element.13.dx_ref, bf16[2688,128]{1,0:T(8,128)(2,1)} %get-tuple-element.14.g_ref, ...), custom_call_target="tpu_custom_call" | custom-call | tf_op jit(solution)/shard_map/pallas_call | solution.py:553

commit v4 on v3

--- a/solution.py
+++ b/solution.py
@@ -31,7 +31,7 @@
 STACK = 2 * PIECE
 SHARE = 3 * PIECE * D
 CHUNK = 8192
-STEPS = 6
+STEPS = 3
 
 
 def dot(left, right, left_dim, right_dim):
@@ -70,10 +70,9 @@
 
     barrier = pltpu.get_barrier_semaphore()
 
-    def greet(k, carry):
-        pl.semaphore_signal(barrier, inc=1, device_id=at_tensor(peer(k)), device_id_type=MESH)
-        return carry
-    lax.fori_loop(1, N_TENSOR, greet, 0)
+    for shift in range(1, 4):
+        pl.semaphore_signal(barrier, inc=1, device_id=at_tensor(peer(shift)), device_id_type=MESH)
+        pl.semaphore_signal(barrier, inc=1, device_id=at_tensor(peer(4 * shift)), device_id_type=MESH)
     pl.semaphore_signal(barrier, inc=1, device_id=partner, device_id_type=MESH)
     for layer in range(2):
         pl.semaphore_signal(barrier, inc=1, device_id=(up_d, me_t, layer), device_id_type=MESH)
@@ -106,7 +105,7 @@
     rows_of(other, 2)
     rows_of(me_c, me_c)
 
-    pl.semaphore_wait(barrier, N_TENSOR + 4)
+    pl.semaphore_wait(barrier, 11)
 
     def to_partner(src, dst, sems, index=None):
         send = sems.at[0] if index is None else sems.at[0, index]

time: 109 us -> 108 us (level)
  no operation moved by 1% of the time
where the time goes in v4:
time: 108 us
  Pallas kernels  107 us (99%)
    pallas_call x1, Pallas kernels, backward(): pl.pallas_call(kernel, out_shape=(jax.ShapeDtypeStruct((2, TOK, WIDE), BF...  101 us
    pallas_call x1, Pallas kernels, adam(): pl.pallas_call(finish, out_shape=(jax.ShapeDtypeStruct(dx.shape, BF),) +...  6.26 us

profile of v4, /device:TPU:2, one launch (start us, length us, event | category | flops | bytes accessed | tf_op | source)
XLA Modules:
  0.0 107.6 jit_solution(3898318839462048738)
XLA Ops:
  0.6 100.7 %shard_map.119 = (bf16[2,512,128]{2,1,0:T(8,128)(2,1)}, bf16[2688,128]{1,0:T(8,128)(2,1)}, bf16[2688,128]{1,0:T(8,128)(2,1)}) custom-call(bf16[2,512,128]{2,1,0:T(8,128)(2,1)} %bitcast.9, bf16[2,512,128]{2,1,0:T(8,128)(2,1)} %dy_hbm.1, s32[2,256]{1,0:T(2,128)} %bitcast.11, s32[1,2]{1,0:T(1,128)} %bitcast.13, f32[2,256]{1,0:T(2,128)} %bitcast.12, ...), custom_call_target="tpu_custom_call" | custom-call | flops 7516192768 | bytes 31457280 | tf_op jit(solution)/shard_map/pallas_call | solution.py:509
  101.3 6.3 %shard_map.120 = (bf16[2,512,128]{2,1,0:T(8,128)(2,1)}, bf16[1,344064]{1,0:T(2,128)(2,1)}, bf16[1,344064]{1,0:T(2,128)(2,1)}, bf16[1,344064]{1,0:T(2,128)(2,1)}, bf16[1,344064]{1,0:T(2,128)(2,1)}) custom-call(bf16[2,512,128]{2,1,0:T(8,128)(2,1)} %get-tuple-element.13.dx_ref, bf16[2688,128]{1,0:T(8,128)(2,1)} %get-tuple-element.14.g_ref, ...), custom_call_target="tpu_custom_call" | custom-call | tf_op jit(solution)/shard_map/pallas_call | solution.py:552

commit v5 on v4

--- a/solution.py
+++ b/solution.py
@@ -430,17 +430,17 @@
     hidden_grads(0)
     weight_grads_away(0)
     weight_grads_here(0)
+    ring_first(0)
     row_grads(0)
-    ring_first(0)
     own_parts()
     part_copy = to_partner(away, owned.at[me_c], part_sem)
     part_copy.start()
     ring_step(0, 1)
     ring_step(0, 2)
+    ring_step(0, 3)
     to_tokens(0, dxs[1])
     dx_copy = to_partner(dxs.at[other], dxoth, dx_sem)
     dx_copy.start()
-    ring_step(0, 3)
     for piece in ones + zeros + grads:
         piece.drain()
     w_out_ref[...] = flat_w[...].astype(BF)

time: 108 us -> 108 us (level)
  no operation moved by 1% of the time
where the time goes in v5:
time: 108 us
  Pallas kernels  107 us (99%)
    pallas_call x1, Pallas kernels, backward(): pl.pallas_call(kernel, out_shape=(jax.ShapeDtypeStruct((2, TOK, WIDE), BF...  101 us
    pallas_call x1, Pallas kernels, adam(): pl.pallas_call(finish, out_shape=(jax.ShapeDtypeStruct(dx.shape, BF),) +...  6.26 us

profile of v5, /device:TPU:2, one launch (start us, length us, event | category | flops | bytes accessed | tf_op | source)
XLA Modules:
  0.0 108.0 jit_solution(5553919738188564757)
XLA Ops:
  0.6 101.1 %shard_map.119 = (bf16[2,512,128]{2,1,0:T(8,128)(2,1)}, bf16[2688,128]{1,0:T(8,128)(2,1)}, bf16[2688,128]{1,0:T(8,128)(2,1)}) custom-call(bf16[2,512,128]{2,1,0:T(8,128)(2,1)} %bitcast.9, bf16[2,512,128]{2,1,0:T(8,128)(2,1)} %dy_hbm.1, s32[2,256]{1,0:T(2,128)} %bitcast.11, s32[1,2]{1,0:T(1,128)} %bitcast.13, f32[2,256]{1,0:T(2,128)} %bitcast.12, ...), custom_call_target="tpu_custom_call" | custom-call | flops 7516192768 | bytes 31457280 | tf_op jit(solution)/shard_map/pallas_call | solution.py:509
  101.7 6.3 %shard_map.120 = (bf16[2,512,128]{2,1,0:T(8,128)(2,1)}, bf16[1,344064]{1,0:T(2,128)(2,1)}, bf16[1,344064]{1,0:T(2,128)(2,1)}, bf16[1,344064]{1,0:T(2,128)(2,1)}, bf16[1,344064]{1,0:T(2,128)(2,1)}) custom-call(bf16[2,512,128]{2,1,0:T(8,128)(2,1)} %get-tuple-element.13.dx_ref, bf16[2688,128]{1,0:T(8,128)(2,1)} %get-tuple-element.14.g_ref, ...), custom_call_target="tpu_custom_call" | custom-call | tf_op jit(solution)/shard_map/pallas_call | solution.py:552
